TPU v7x, 32 devices: a whole 2x2x4 slice. The times are simulated.
32 devices in a mesh: ccd: 4 (over y, core), tile: 8 (over z, x).
Axes of the slice: x: 2, y: 2, z: 4, core: 2. Of those that a mesh axis runs over, the one named last changes fastest.
Arguments:
- exposures: float32 [8, 2048, 4096], P('tile', 'ccd'), may hold values from -6 to 6
- interp: bfloat16 [8, 32, 256, 128], P('tile'), may hold values from -0.375 to 0.375
- col_offsets: int32 [8, 32], P('tile'), may hold values from 0 to 30
- template: float32 [2048, 4096], P('ccd', 'tile'), may hold values from -6 to 6
- coef_table: float32 [8, 4, 3, 3], replicated, may hold values from -3 to 3
- coef_index: int32 [8, 4, 8], replicated, may hold values from 0 to 3
- intersection: int32 [8, 4, 8], replicated, may hold values 0 or 1
Outputs:
- difference: float32 [8, 2048, 4096], P('tile', 'ccd')
All inputs are finite; a program needn't handle non-finite values.
Results may differ from a plain program's by a relative error of at most 0.0029.
Values sent between devices are 32-bit elements; how exact they have to be, the bound alone decides.
A program may use at most 128 MiB of HBM per device.

v0:
```python
import functools

import jax
import jax.numpy as jnp
import ml_dtypes
import numpy as np
from jax import lax
from jax.experimental import pallas as pl
from jax.experimental.pallas import tpu as pltpu
from jax.sharding import PartitionSpec as P

HALF = 10
KSETS = 4
SIGMAS = (1.5, 3.0, 5.0)
HALO = 16
EDGE = 128
BAND = 128
CHUNKS = 2
LINES = 128


def basis_taps():
    positions = np.arange(-HALF, HALF + 1).astype(np.float64)
    kernels = []
    for sigma_value in SIGMAS:
        gauss = np.exp(-0.5 * (positions / sigma_value) ** 2)
        kernels.append(gauss / np.sum(gauss))
    return kernels


def smoothing_gains():
    near = [taps.astype(ml_dtypes.bfloat16).astype(np.float64) for taps in basis_taps()]
    return [1.0 / np.sum(taps) ** 2 for taps in near]


def banded(b, rows, cols, shift, first=0):
    shape = (rows, cols)
    distance = (
        lax.broadcasted_iota(jnp.int32, shape, 1)
        - lax.broadcasted_iota(jnp.int32, shape, 0)
        - (shift + first)
    )
    away = distance.astype(jnp.float32)
    taps = jnp.exp(away * away * (-0.5 / SIGMAS[b] ** 2)) * basis_taps()[b][HALF]
    return jnp.where(jnp.abs(away) <= HALF, taps, 0.0).astype(jnp.bfloat16)


def inner_size(count):
    best = 1
    for size in range(1, count + 1):
        if count % size == 0 and size * size <= count:
            best = size
    return best


def arrival_events(count):
    inner = inner_size(count)
    events = []
    for me in range(count):
        z, x = divmod(me, inner)
        near = sorted(range(count // inner), key=lambda other: (abs(other - z), other))
        keys = []
        for q in range(count):
            if q == me:
                continue
            qz, qx = divmod(q, inner)
            away = abs(qz - z)
            time = away if qx == x else max(near.index(qz), away) + abs(qx - x)
            keys.append((time, qx != x, q))
        events.append([q * CHUNKS + c for _, _, q in sorted(keys) for c in range(CHUNKS)])
    return events


DIGIT = 256
PER_WORD = 3


def arrival_codes(count):
    codes = []
    for events in arrival_events(count):
        assert len(events) == (count - 1) * CHUNKS
        left = {q: CHUNKS for q in range(count)}
        digits = []
        for event in events:
            left[event // CHUNKS] -= 1
            digits.append(event * 2 + (left[event // CHUNKS] == 0))
        codes.append([
            sum(int(v) * DIGIT**i for i, v in enumerate(digits[first : first + PER_WORD]))
            for first in range(0, len(digits), PER_WORD)
        ])
    return codes


def model_kernel(
    count, ccd_count, template, weights, out,
    strip, down, across, load_sem, send_sem, recv_sem, hsend_sem, hrecv_sem,
):
    me = lax.axis_index("tile")
    row = lax.axis_index("ccd")
    inner = inner_size(count)
    outer = count // inner
    z, x = me // inner, me % inner
    rows, patch_cols = template.shape
    cols = out.shape[1]
    part = rows // CHUNKS

    targets = (me - inner, me + inner, me - 1, me + 1)
    there = (z > 0, z < outer - 1, x > 0, x < inner - 1)
    halo_there = (row > 0, row < ccd_count - 1)

    load = pltpu.make_async_copy(template, strip.at[me, pl.ds(HALO, rows)], load_sem)
    load.start()

    barrier = pltpu.get_barrier_semaphore()
    total = jnp.int32(0)
    for target, exists in zip(targets, there):
        @pl.when(exists)
        def _():
            pl.semaphore_signal(barrier, inc=1, device_id=(row, target))
        total = total + exists.astype(jnp.int32)
    for step, exists in zip((-1, 1), halo_there):
        @pl.when(exists)
        def _():
            pl.semaphore_signal(barrier, inc=1, device_id=(row + step, me))
        total = total + exists.astype(jnp.int32)
    pl.semaphore_wait(barrier, total)

    def send(q, c, d, own):
        piece = pl.ds(pl.multiple_of(HALO + c * part, HALO), part)
        return pltpu.make_async_remote_copy(
            src_ref=template.at[pl.ds(c * part, part)] if own else strip.at[q, piece],
            dst_ref=strip.at[q, piece],
            send_sem=send_sem.at[d, q, c],
            recv_sem=recv_sem.at[q, c],
            device_id=(row, targets[d]),
        )

    def halo(q, d):
        source = pl.ds(HALO, HALO) if d == 0 else pl.ds(rows, HALO)
        target = pl.ds(HALO + rows, HALO) if d == 0 else pl.ds(0, HALO)
        return pltpu.make_async_remote_copy(
            src_ref=strip.at[q, source],
            dst_ref=strip.at[q, target],
            send_sem=hsend_sem.at[d, q],
            recv_sem=hrecv_sem.at[d, q],
            device_id=(row + (-1 if d == 0 else 1), me),
        )

    for c in range(CHUNKS):
        for d in range(4):
            @pl.when(there[d])
            def _():
                send(me, c, d, True).start()
    load.wait()
    for d in range(2):
        @pl.when(halo_there[d])
        def _():
            halo(me, d).start()

    @pl.when(row == 0)
    def _():
        for q in range(count):
            strip[q, 0:HALO, :] = jnp.zeros((HALO, patch_cols), jnp.float32)

    @pl.when(row == ccd_count - 1)
    def _():
        for q in range(count):
            strip[q, rows + HALO : rows + 2 * HALO, :] = jnp.zeros((HALO, patch_cols), jnp.float32)

    def clear(r, carry):
        out[pl.ds(pl.multiple_of(r * HALO, HALO), HALO), :] = jnp.zeros((HALO, cols), jnp.float32)
        return carry

    lax.fori_loop(0, rows // HALO, clear, 0)

    def add_model(q):
        first = pl.multiple_of(q * patch_cols, EDGE)
        wide = patch_cols + 2 * EDGE
        left = pl.multiple_of(jnp.maximum(first - EDGE, 0), EDGE)
        right = pl.multiple_of(jnp.minimum(first + patch_cols, cols - EDGE), EDGE)

        def band(r, carry):
            at = pl.multiple_of(r * BAND, BAND)
            lines = pl.ds(at, BAND)
            pixel = strip[q, pl.ds(at, BAND + 2 * HALO), :].astype(jnp.bfloat16)
            tall = jnp.dot(down[...], pixel, preferred_element_type=jnp.float32)
            tall = tall.astype(jnp.bfloat16)
            v = (
                lax.broadcasted_iota(jnp.int32, (BAND, wide), 0) + r * BAND
            ).astype(jnp.float32) * (2.0 / rows) - (rows - 1) / rows
            model = None
            for b in range(3):
                flat = jnp.dot(
                    tall[b * BAND : (b + 1) * BAND], across[b], preferred_element_type=jnp.float32
                )
                const = weights[b : b + 1, pl.ds(first, wide)]
                slope = weights[3 + b : 4 + b, pl.ds(first, wide)]
                term = (const + slope * v) * flat
                model = term if model is None else model + term
            out[lines, pl.ds(first, patch_cols)] += model[:, EDGE : EDGE + patch_cols]
            out[lines, pl.ds(left, EDGE)] += model[:, :EDGE]
            out[lines, pl.ds(right, EDGE)] += model[:, EDGE + patch_cols :]
            return carry

        lax.fori_loop(0, rows // BAND, band, 0)

    def halos_in(q):
        for d in range(2):
            @pl.when(halo_there[1 - d])
            def _():
                halo(q, d).wait_recv()

    for b in range(3):
        down[b * BAND : (b + 1) * BAND, :] = banded(b, BAND, BAND + 2 * HALO, HALO)

        def fill(i, carry):
            first = pl.multiple_of(i * HALO, HALO)
            across[b, pl.ds(first, HALO), :] = banded(
                b, HALO, patch_cols + 2 * EDGE, EDGE, i * HALO
            )
            return carry

        lax.fori_loop(0, patch_cols // HALO, fill, 0)

    halos_in(me)
    add_model(me)

    def paths(q, c):
        qz, qx = q // inner, q % inner
        along = qx == x
        return (
            along & (qz >= z) & there[0],
            along & (qz <= z) & there[1],
            (qx >= x) & there[2],
            (qx <= x) & there[3],
        )

    table = arrival_codes(count)
    words = []
    for w in range(len(table[0])):
        word = jnp.int32(0)
        for i in range(count):
            word = jnp.where(me == i, jnp.int32(table[i][w]), word)
        words.append(word)

    def arrive(_, words):
        words = list(words)
        digit = words[0] % DIGIT
        for w in range(len(words)):
            words[w] = words[w] // DIGIT
            if w + 1 < len(words):
                words[w] = words[w] + (words[w + 1] % DIGIT) * DIGIT ** (PER_WORD - 1)
        done, event = digit % 2, digit // 2
        q, c = event // CHUNKS, event % CHUNKS
        send(q, c, 0, False).wait_recv()
        onward = paths(q, c)
        for d in range(4):
            @pl.when(onward[d])
            def _():
                send(q, c, d, False).start()
        for d in range(2):
            @pl.when((c == (0 if d == 0 else CHUNKS - 1)) & halo_there[d])
            def _():
                halo(q, d).start()

        @pl.when(done == 1)
        def _():
            halos_in(q)
            add_model(q)

        return tuple(words)

    lax.fori_loop(0, (count - 1) * CHUNKS, arrive, tuple(words))

    def drain(event, carry):
        q, c = event // CHUNKS, event % CHUNKS
        onward = paths(q, c)
        for d in range(4):
            @pl.when(onward[d])
            def _():
                send(q, c, d, False).wait_send()
        for d in range(2):
            @pl.when((c == 0) & halo_there[d])
            def _():
                halo(q, d).wait_send()
        return carry

    lax.fori_loop(0, count * CHUNKS, drain, 0)


def difference_kernel(offsets, exposure, mats, model, weights, out, pixels):
    blocks, depth, block = mats.shape
    pixels[...] = exposure[...].astype(jnp.bfloat16)
    for j in range(blocks):
        start = pl.multiple_of(offsets[j] * block, block)
        value = jnp.dot(
            pixels[:, pl.ds(start, depth)], mats[j], preferred_element_type=jnp.float32
        )
        here = slice(j * block, (j + 1) * block)
        covered = weights[6:7, EDGE + j * block : EDGE + (j + 1) * block]
        out[:, here] = value * covered - model[:, here]


def on_device(exposures, interp, col_offsets, template, coef_table, coef_index, intersection):
    rows, cols = exposures.shape[1:]
    patch_cols = template.shape[1]
    count, ccd_count = lax.axis_size("tile"), lax.axis_size("ccd")
    patch_row = lax.axis_index("ccd")
    my_epoch = lax.axis_index("tile")
    gains = smoothing_gains()

    set_ids = coef_index[my_epoch, patch_row]
    set_pick = (set_ids[:, None] == jnp.arange(KSETS)[None, :]).astype(jnp.float32)
    coef = jnp.sum(set_pick[:, :, None, None] * coef_table[my_epoch][None], axis=1)
    covered = intersection[my_epoch, patch_row].astype(jnp.float32)
    coef = coef * covered[:, None, None] * jnp.asarray(gains, jnp.float32)[None, :, None]
    u = (jnp.arange(patch_cols).astype(jnp.float32) - (patch_cols - 1) / 2.0) / (patch_cols / 2.0)
    spread = coef.transpose(1, 2, 0)[:, :, :, None]
    const = (spread[:, 0] + spread[:, 1] * u[None, None, :]).reshape(3, cols)
    slope = jnp.broadcast_to(spread[:, 2], (3, count, patch_cols)).reshape(3, cols)
    cover = jnp.broadcast_to(covered[None, :, None], (2, count, patch_cols)).reshape(2, cols)
    weights = jnp.pad(jnp.concatenate([const, slope, cover]), ((0, 0), (EDGE, EDGE)))

    in_hbm = pl.BlockSpec(memory_space=pltpu.HBM)
    vmem = pl.BlockSpec(memory_space=pltpu.VMEM)
    model = pl.pallas_call(
        functools.partial(model_kernel, count, ccd_count),
        out_shape=jax.ShapeDtypeStruct((rows, cols), jnp.float32),
        in_specs=[in_hbm, vmem],
        out_specs=vmem,
        scratch_shapes=[
            pltpu.VMEM((count, rows + 2 * HALO, patch_cols), jnp.float32),
            pltpu.VMEM((3 * BAND, BAND + 2 * HALO), jnp.bfloat16),
            pltpu.VMEM((3, patch_cols, patch_cols + 2 * EDGE), jnp.bfloat16),
            pltpu.SemaphoreType.DMA,
            pltpu.SemaphoreType.DMA((4, count, CHUNKS)),
            pltpu.SemaphoreType.DMA((count, CHUNKS)),
            pltpu.SemaphoreType.DMA((2, count)),
            pltpu.SemaphoreType.DMA((2, count)),
        ],
        compiler_params=pltpu.CompilerParams(
            collective_id=0, has_side_effects=True, vmem_limit_bytes=32 * 2**20
        ),
    )(template, weights)

    blocks, depth, block = interp.shape[1:]
    lines = min(LINES, rows)
    result = pl.pallas_call(
        difference_kernel,
        grid=(rows // lines,),
        out_shape=jax.ShapeDtypeStruct((rows, cols), jnp.float32),
        in_specs=[
            pl.BlockSpec(memory_space=pltpu.SMEM),
            pl.BlockSpec((lines, cols), lambda i: (i, 0)),
            pl.BlockSpec((blocks, depth, block), lambda i: (0, 0, 0)),
            pl.BlockSpec((lines, cols), lambda i: (i, 0)),
            pl.BlockSpec(weights.shape, lambda i: (0, 0)),
        ],
        out_specs=pl.BlockSpec((lines, cols), lambda i: (i, 0)),
        scratch_shapes=[pltpu.VMEM((lines, cols), jnp.bfloat16)],
        compiler_params=pltpu.CompilerParams(vmem_limit_bytes=32 * 2**20),
    )(col_offsets[0], exposures[0], interp[0], model, weights)
    return result[None]


def solution(mesh):
    placed = (
        P("tile", "ccd", None),
        P("tile", None, None, None),
        P("tile", None),
        P("ccd", "tile"),
        P(),
        P(),
        P(),
    )
    return jax.shard_map(
        on_device, mesh=mesh, in_specs=placed, out_specs=P("tile", "ccd", None), check_vma=False
    )
```

profile of v0, /device:TPU:1, one launch (start us, length us, event | category | flops | bytes accessed | tf_op | source)
XLA Modules:
  0.0 110.6 jit_solution(4288420387409853821)
XLA Ops:
  0.0 0.0 copy-start
  0.0 0.0 copy-start.2
  0.0 0.9 fusion.2
  0.9 0.1 broadcast_bitcast_fusion.3
  1.0 0.0 copy-done
  1.0 0.1 constant_dynamic-slice_fusion.1
  1.1 0.2 copy.13
  1.2 0.0 copy-start.1
  1.2 0.1 multiply_reduce_fusion
  1.3 0.9 multiply_bitcast_fusion
  2.3 0.1 broadcast_bitcast_fusion.2
  2.4 0.1 broadcast_bitcast_fusion
  2.5 0.1 broadcast_bitcast_fusion.1
  2.7 0.0 copy-start.3
  2.7 1.6 %copy-done.3 = f32[512,512]{1,0:T(8,128)S(1)} copy-done((f32[512,512]{1,0:T(8,128)S(1)}, f32[512,512]{1,0:T(8,128)}, u32[]{:S(2)}) %copy-start.3) | copy-done | bytes 1048600
  4.3 0.0 copy-start.4
  4.3 100.3 %shard_map.82.model = f32[512,4096]{1,0:T(8,128)S(1)} custom-call(f32[512,512]{1,0:T(8,128)S(1)} %copy-done.3, f32[8,4352]{1,0:T(8,128)S(1)} %select_maximum_fusion.weights), custom_call_target="tpu_custom_call" | custom-call | tf_op jit(solution)/shard_map/pallas_call | solution.py:326
  104.6 0.0 copy-done.2
  104.7 0.0 copy-done.1
  104.7 0.0 copy-done.4
  104.7 5.9 %shard_map.83 = f32[512,4096]{1,0:T(8,128)} custom-call(s32[32]{0:T(128)S(1)} %bitcast.40, f32[512,4096]{1,0:T(8,128)S(1)} %bitcast.38, bf16[32,256,128]{2,1,0:T(8,128)(2,1)S(1)} %bitcast.39, f32[512,4096]{1,0:T(8,128)S(1)} %shard_map.82.model, f32[8,4352]{1,0:T(8,128)S(1)} %select_maximum_fusion.weights), custom_call_target="tpu_custom_call" | custom-call | tf_op jit(solution)/shard_map/pallas_call | solution.py:348
  (15 shorter events, 0.3 us)
Async XLA Ops:
  0.0 1.0 copy-start
  0.0 104.6 %copy-start.2 = (bf16[1,32,256,128]{3,2,1,0:T(8,128)(2,1)S(1)}, bf16[1,32,256,128]{3,2,1,0:T(8,128)(2,1)}, u32[]{:S(2)}) copy-start(bf16[1,32,256,128]{3,2,1,0:T(8,128)(2,1)} %param.9) | copy-start | bytes 6291460
  1.2 103.4 %copy-start.1 = (f32[1,512,4096]{2,1,0:T(8,128)S(1)}, f32[1,512,4096]{2,1,0:T(8,128)}, u32[]{:S(2)}) copy-start(f32[1,512,4096]{2,1,0:T(8,128)} %param.8) | copy-start | bytes 25165828
  2.7 1.6 %copy-start.3 = (f32[512,512]{1,0:T(8,128)S(1)}, f32[512,512]{1,0:T(8,128)}, u32[]{:S(2)}) copy-start(f32[512,512]{1,0:T(8,128)} %template.1) | copy-start | bytes 3145732
  4.3 100.4 %copy-start.4 = (s32[1,32]{1,0:T(1,128)S(1)}, s32[1,32]{1,0:T(1,128)}, u32[]{:S(2)}) copy-start(s32[1,32]{1,0:T(1,128)} %param.10) | copy-start | bytes 388
where the time goes:
time: 111 us
  Pallas kernels  106 us (95%)
  local copies, waits for them, and re-layouts  2.29 us (2%)
  other arithmetic  1.92 us (2%)
    pallas_call x1, Pallas kernels, on_device(): pl.pallas_call(functools.partial(model_kernel, count, ccd_count), out_sha...  100 us
    pallas_call x1, Pallas kernels, on_device(): pl.pallas_call(difference_kernel, grid=(rows // lines,), out_shape=jax.Sh...  5.89 us

commit v1 on v0

--- a/solution.py
+++ b/solution.py
@@ -1,4 +1,5 @@
 import functools
+import heapq
 
 import jax
 import jax.numpy as jnp
@@ -17,6 +18,7 @@
 BAND = 128
 CHUNKS = 2
 LINES = 128
+STORES = 8
 
 
 def basis_taps():
@@ -53,21 +55,47 @@
     return best
 
 
+def turns(d, qz, c, outer):
+    late = c >= CHUNKS // 2
+    ends = ((d == 0) & (qz == outer - 1)) | ((d == outer - 1) & (qz == 0))
+    inside = (d > 0) & (d < outer - 1) & ((qz == d - 1) | (qz == d + 1))
+    return (ends & late) | (inside & (late | (qz == 0) | (qz == outer - 1)))
+
+
+def paths(me, q, c, count):
+    inner = inner_size(count)
+    outer = count // inner
+    z, x = me // inner, me % inner
+    qz, qx = q // inner, q % inner
+    own = qx == x
+    across = (qz == z) | (turns(z, qz, c, outer) ^ True)
+    return (
+        (z > 0) & (qz >= z) & (own | turns(z - 1, qz, c, outer)),
+        (z < outer - 1) & (qz <= z) & (own | turns(z + 1, qz, c, outer)),
+        across & (qx >= x) & (x > 0),
+        across & (qx <= x) & (x < inner - 1),
+    )
+
+
 def arrival_events(count):
     inner = inner_size(count)
-    events = []
-    for me in range(count):
-        z, x = divmod(me, inner)
-        near = sorted(range(count // inner), key=lambda other: (abs(other - z), other))
-        keys = []
-        for q in range(count):
-            if q == me:
-                continue
-            qz, qx = divmod(q, inner)
-            away = abs(qz - z)
-            time = away if qx == x else max(near.index(qz), away) + abs(qx - x)
-            keys.append((time, qx != x, q))
-        events.append([q * CHUNKS + c for _, _, q in sorted(keys) for c in range(CHUNKS)])
+    steps = (-inner, inner, -1, 1)
+    free, order = {}, 0
+    queue = [(0, False, me, me, c, me * CHUNKS + c) for me in range(count) for c in range(CHUNKS)]
+    order = len(queue)
+    heapq.heapify(queue)
+    events = [[] for _ in range(count)]
+    while queue:
+        time, _, me, q, c, _ = heapq.heappop(queue)
+        if q != me:
+            events[me].append(q * CHUNKS + c)
+        for d, go in enumerate(paths(me, q, c, count)):
+            if go:
+                done = max(free.get((me, d), 0), time) + 1
+                free[me, d] = done
+                to = me + steps[d]
+                heapq.heappush(queue, (done, (q - to) % inner != 0, to, q, c, order))
+                order += 1
     return events
 
 
@@ -91,9 +119,10 @@
     return codes
 
 
-def model_kernel(
-    count, ccd_count, template, weights, out,
-    strip, down, across, load_sem, send_sem, recv_sem, hsend_sem, hrecv_sem,
+def strip_kernel(
+    count, ccd_count, template, exposure, interp, offset_in, coef_in, index_in, cover_in, out,
+    strip, down, across, weights, lines, pixels, mats, offsets, coef, index, cover,
+    load_sem, line_sem, small_sem, send_sem, recv_sem, hsend_sem, hrecv_sem,
 ):
     me = lax.axis_index("tile")
     row = lax.axis_index("ccd")
@@ -107,9 +136,6 @@
     targets = (me - inner, me + inner, me - 1, me + 1)
     there = (z > 0, z < outer - 1, x > 0, x < inner - 1)
     halo_there = (row > 0, row < ccd_count - 1)
-
-    load = pltpu.make_async_copy(template, strip.at[me, pl.ds(HALO, rows)], load_sem)
-    load.start()
 
     barrier = pltpu.get_barrier_semaphore()
     total = jnp.int32(0)
@@ -123,6 +149,24 @@
         def _():
             pl.semaphore_signal(barrier, inc=1, device_id=(row + step, me))
         total = total + exists.astype(jnp.int32)
+
+    load = pltpu.make_async_copy(template, strip.at[me, pl.ds(HALO, rows)], load_sem)
+    load.start()
+    small = [
+        pltpu.make_async_copy(source, target, small_sem.at[i])
+        for i, (source, target) in enumerate(
+            [(offset_in, offsets), (coef_in, coef), (index_in, index), (cover_in, cover), (interp, mats)]
+        )
+    ]
+    for copy in small:
+        copy.start()
+
+    def line_copy(i, slot):
+        return pltpu.make_async_copy(
+            exposure.at[pl.ds(pl.multiple_of(i * LINES, LINES), LINES)], lines.at[slot], line_sem.at[slot]
+        )
+
+    line_copy(0, 0).start()
     pl.semaphore_wait(barrier, total)
 
     def send(q, c, d, own):
@@ -167,11 +211,56 @@
         for q in range(count):
             strip[q, rows + HALO : rows + 2 * HALO, :] = jnp.zeros((HALO, patch_cols), jnp.float32)
 
-    def clear(r, carry):
-        out[pl.ds(pl.multiple_of(r * HALO, HALO), HALO), :] = jnp.zeros((HALO, cols), jnp.float32)
+    for copy in small:
+        copy.wait()
+
+    blocks, depth, block = mats.shape
+
+    def warp(i, carry):
+        slot = i % 2
+        line_copy(i, slot).wait()
+
+        @pl.when(i + 1 < rows // LINES)
+        def _():
+            line_copy(i + 1, 1 - slot).start()
+
+        for j in range(blocks):
+            pixels[j] = lines[slot, :, j * block : (j + 1) * block].astype(jnp.bfloat16)
+        here = pl.ds(pl.multiple_of(i * LINES, LINES), LINES)
+        for j in range(blocks):
+            start = offsets[j]
+            window = [pixels[start + k] for k in range(depth // block)]
+            value = jnp.dot(
+                jnp.concatenate(window, axis=1), mats[j], preferred_element_type=jnp.float32
+            )
+            covered = cover[me * (ccd_count * count) + row * count + j * block // patch_cols]
+            out[here, j * block : (j + 1) * block] = value * covered.astype(jnp.float32)
         return carry
 
-    lax.fori_loop(0, rows // HALO, clear, 0)
+    lax.fori_loop(0, rows // LINES, warp, 0)
+
+    gains = smoothing_gains()
+    u = (
+        lax.broadcasted_iota(jnp.int32, (1, patch_cols), 1).astype(jnp.float32) * (2.0 / patch_cols)
+        - (patch_cols - 1) / patch_cols
+    )
+    weights[...] = jnp.zeros(weights.shape, jnp.float32)
+    for q in range(count):
+        spot = me * (ccd_count * count) + row * count + q
+        chosen = index[spot]
+        covered = cover[spot].astype(jnp.float32)
+        here = slice(EDGE + q * patch_cols, EDGE + (q + 1) * patch_cols)
+        for b in range(3):
+            terms = []
+            for k in range(3):
+                sets = [coef[me * (KSETS * 9) + i * 9 + b * 3 + k] for i in range(KSETS)]
+                term = sets[0]
+                for i in range(1, KSETS):
+                    term = jnp.where(chosen == i, sets[i], term)
+                terms.append(term * covered * float(gains[b]))
+            const, slope, lift = terms
+            weights[b : b + 1, here] = const + slope * u
+            weights[3 + b : 4 + b, here] = jnp.full((1, patch_cols), lift, jnp.float32)
 
     def add_model(q):
         first = pl.multiple_of(q * patch_cols, EDGE)
@@ -181,7 +270,7 @@
 
         def band(r, carry):
             at = pl.multiple_of(r * BAND, BAND)
-            lines = pl.ds(at, BAND)
+            here = pl.ds(at, BAND)
             pixel = strip[q, pl.ds(at, BAND + 2 * HALO), :].astype(jnp.bfloat16)
             tall = jnp.dot(down[...], pixel, preferred_element_type=jnp.float32)
             tall = tall.astype(jnp.bfloat16)
@@ -197,9 +286,9 @@
                 slope = weights[3 + b : 4 + b, pl.ds(first, wide)]
                 term = (const + slope * v) * flat
                 model = term if model is None else model + term
-            out[lines, pl.ds(first, patch_cols)] += model[:, EDGE : EDGE + patch_cols]
-            out[lines, pl.ds(left, EDGE)] += model[:, :EDGE]
-            out[lines, pl.ds(right, EDGE)] += model[:, EDGE + patch_cols :]
+            out[here, pl.ds(first, patch_cols)] -= model[:, EDGE : EDGE + patch_cols]
+            out[here, pl.ds(left, EDGE)] -= model[:, :EDGE]
+            out[here, pl.ds(right, EDGE)] -= model[:, EDGE + patch_cols :]
             return carry
 
         lax.fori_loop(0, rows // BAND, band, 0)
@@ -224,16 +313,6 @@
 
     halos_in(me)
     add_model(me)
-
-    def paths(q, c):
-        qz, qx = q // inner, q % inner
-        along = qx == x
-        return (
-            along & (qz >= z) & there[0],
-            along & (qz <= z) & there[1],
-            (qx >= x) & there[2],
-            (qx <= x) & there[3],
-        )
 
     table = arrival_codes(count)
     words = []
@@ -253,7 +332,7 @@
         done, event = digit % 2, digit // 2
         q, c = event // CHUNKS, event % CHUNKS
         send(q, c, 0, False).wait_recv()
-        onward = paths(q, c)
+        onward = paths(me, q, c, count)
         for d in range(4):
             @pl.when(onward[d])
             def _():
@@ -274,7 +353,7 @@
 
     def drain(event, carry):
         q, c = event // CHUNKS, event % CHUNKS
-        onward = paths(q, c)
+        onward = paths(me, q, c, count)
         for d in range(4):
             @pl.when(onward[d])
             def _():
@@ -288,78 +367,62 @@
     lax.fori_loop(0, count * CHUNKS, drain, 0)
 
 
-def difference_kernel(offsets, exposure, mats, model, weights, out, pixels):
-    blocks, depth, block = mats.shape
-    pixels[...] = exposure[...].astype(jnp.bfloat16)
-    for j in range(blocks):
-        start = pl.multiple_of(offsets[j] * block, block)
-        value = jnp.dot(
-            pixels[:, pl.ds(start, depth)], mats[j], preferred_element_type=jnp.float32
-        )
-        here = slice(j * block, (j + 1) * block)
-        covered = weights[6:7, EDGE + j * block : EDGE + (j + 1) * block]
-        out[:, here] = value * covered - model[:, here]
+def store_kernel(value, out, sem):
+    rows = value.shape[0] // STORES
+    copies = [
+        pltpu.make_async_copy(value.at[pl.ds(i * rows, rows)], out.at[pl.ds(i * rows, rows)], sem.at[i])
+        for i in range(STORES)
+    ]
+    for copy in copies:
+        copy.start()
+    for copy in copies:
+        copy.wait()
 
 
 def on_device(exposures, interp, col_offsets, template, coef_table, coef_index, intersection):
     rows, cols = exposures.shape[1:]
     patch_cols = template.shape[1]
     count, ccd_count = lax.axis_size("tile"), lax.axis_size("ccd")
-    patch_row = lax.axis_index("ccd")
-    my_epoch = lax.axis_index("tile")
-    gains = smoothing_gains()
-
-    set_ids = coef_index[my_epoch, patch_row]
-    set_pick = (set_ids[:, None] == jnp.arange(KSETS)[None, :]).astype(jnp.float32)
-    coef = jnp.sum(set_pick[:, :, None, None] * coef_table[my_epoch][None], axis=1)
-    covered = intersection[my_epoch, patch_row].astype(jnp.float32)
-    coef = coef * covered[:, None, None] * jnp.asarray(gains, jnp.float32)[None, :, None]
-    u = (jnp.arange(patch_cols).astype(jnp.float32) - (patch_cols - 1) / 2.0) / (patch_cols / 2.0)
-    spread = coef.transpose(1, 2, 0)[:, :, :, None]
-    const = (spread[:, 0] + spread[:, 1] * u[None, None, :]).reshape(3, cols)
-    slope = jnp.broadcast_to(spread[:, 2], (3, count, patch_cols)).reshape(3, cols)
-    cover = jnp.broadcast_to(covered[None, :, None], (2, count, patch_cols)).reshape(2, cols)
-    weights = jnp.pad(jnp.concatenate([const, slope, cover]), ((0, 0), (EDGE, EDGE)))
+    blocks, depth, block = interp.shape[1:]
+    small = [coef_table.reshape(-1), coef_index.reshape(-1), intersection.reshape(-1)]
 
     in_hbm = pl.BlockSpec(memory_space=pltpu.HBM)
     vmem = pl.BlockSpec(memory_space=pltpu.VMEM)
-    model = pl.pallas_call(
-        functools.partial(model_kernel, count, ccd_count),
+    value = pl.pallas_call(
+        functools.partial(strip_kernel, count, ccd_count),
         out_shape=jax.ShapeDtypeStruct((rows, cols), jnp.float32),
-        in_specs=[in_hbm, vmem],
+        in_specs=[in_hbm] * 7,
         out_specs=vmem,
         scratch_shapes=[
             pltpu.VMEM((count, rows + 2 * HALO, patch_cols), jnp.float32),
             pltpu.VMEM((3 * BAND, BAND + 2 * HALO), jnp.bfloat16),
             pltpu.VMEM((3, patch_cols, patch_cols + 2 * EDGE), jnp.bfloat16),
+            pltpu.VMEM((8, cols + 2 * EDGE), jnp.float32),
+            pltpu.VMEM((2, LINES, cols), jnp.float32),
+            pltpu.VMEM((blocks, LINES, block), jnp.bfloat16),
+            pltpu.VMEM((blocks, depth, block), jnp.bfloat16),
+            pltpu.SMEM((blocks,), jnp.int32),
+            *[pltpu.SMEM(array.shape, array.dtype) for array in small],
             pltpu.SemaphoreType.DMA,
+            pltpu.SemaphoreType.DMA((2,)),
+            pltpu.SemaphoreType.DMA((5,)),
             pltpu.SemaphoreType.DMA((4, count, CHUNKS)),
             pltpu.SemaphoreType.DMA((count, CHUNKS)),
             pltpu.SemaphoreType.DMA((2, count)),
             pltpu.SemaphoreType.DMA((2, count)),
         ],
         compiler_params=pltpu.CompilerParams(
-            collective_id=0, has_side_effects=True, vmem_limit_bytes=32 * 2**20
+            collective_id=0, has_side_effects=True, vmem_limit_bytes=40 * 2**20
         ),
-    )(template, weights)
-
-    blocks, depth, block = interp.shape[1:]
-    lines = min(LINES, rows)
+    )(template, exposures[0], interp[0], col_offsets[0], *small)
     result = pl.pallas_call(
-        difference_kernel,
-        grid=(rows // lines,),
+        store_kernel,
         out_shape=jax.ShapeDtypeStruct((rows, cols), jnp.float32),
-        in_specs=[
-            pl.BlockSpec(memory_space=pltpu.SMEM),
-            pl.BlockSpec((lines, cols), lambda i: (i, 0)),
-            pl.BlockSpec((blocks, depth, block), lambda i: (0, 0, 0)),
-            pl.BlockSpec((lines, cols), lambda i: (i, 0)),
-            pl.BlockSpec(weights.shape, lambda i: (0, 0)),
-        ],
-        out_specs=pl.BlockSpec((lines, cols), lambda i: (i, 0)),
-        scratch_shapes=[pltpu.VMEM((lines, cols), jnp.bfloat16)],
-        compiler_params=pltpu.CompilerParams(vmem_limit_bytes=32 * 2**20),
-    )(col_offsets[0], exposures[0], interp[0], model, weights)
+        in_specs=[vmem],
+        out_specs=in_hbm,
+        scratch_shapes=[pltpu.SemaphoreType.DMA((STORES,))],
+        compiler_params=pltpu.CompilerParams(vmem_limit_bytes=2**20),
+    )(value)
     return result[None]
 
 

time: 111 us -> 101 us (0.910)
  Pallas kernels: 106 us -> 94.4 us
  local copies, waits for them, and re-layouts: 2.29 us -> 6.14 us
  other arithmetic: 1.92 us -> 0 us
    pallas_call x2, Pallas kernels: 106 us -> 94.4 us  [the longest x1 91 us: on_device(): pl.pallas_call(functools.partial(strip_kernel, count, ccd_count), out_sha...]
    unnamed x23 -> x7, local copies, waits for them, and re-layouts: 2.04 us -> 4.34 us
    reshape x0 -> x3, local copies, waits for them, and re-layouts: none -> 1.8 us  [the longest x1 0.81 us: on_device(): intersection.reshape(-1)]
where the time goes in v1:
time: 101 us
  Pallas kernels  94.4 us (93%)
  local copies, waits for them, and re-layouts  6.14 us (6%)
    pallas_call x1, Pallas kernels, on_device(): pl.pallas_call(functools.partial(strip_kernel, count, ccd_count), out_sha...  91 us
    unnamed x7, local copies, waits for them, and re-layouts  4.34 us
    pallas_call x1, Pallas kernels, on_device(): pl.pallas_call(store_kernel, out_shape=jax.ShapeDtypeStruct((rows, cols),...  3.37 us

profile of v1, /device:TPU:1, one launch (start us, length us, event | category | flops | bytes accessed | tf_op | source)
XLA Modules:
  0.0 100.5 jit_solution(10475648808311091085)
XLA Ops:
  0.0 0.8 reshape.10.index_in
  0.8 0.8 reshape.11.cover_in
  1.6 0.9 copy.8
  2.5 0.2 reshape.9.coef_in
  2.7 0.0 copy-start
  2.7 1.6 %copy-done = bf16[1,32,256,128]{3,2,1,0:T(8,128)(2,1)S(1)} copy-done((bf16[1,32,256,128]{3,2,1,0:T(8,128)(2,1)S(1)}, bf16[1,32,256,128]{3,2,1,0:T(8,128)(2,1)}, u32[]{:S(2)}) %copy-start) | copy-done | bytes 2097176
  4.3 0.0 copy-start.1
  4.3 1.2 %copy-done.1 = f32[512,512]{1,0:T(8,128)S(1)} copy-done((f32[512,512]{1,0:T(8,128)S(1)}, f32[512,512]{1,0:T(8,128)}, u32[]{:S(2)}) %copy-start.1) | copy-done | bytes 1048600
  5.5 0.0 copy-start.2
  5.5 0.7 copy-done.2
  6.2 91.0 %shard_map.73.value = f32[512,4096]{1,0:T(8,128)S(1)} custom-call(f32[512,512]{1,0:T(8,128)S(1)} %copy-done.1, f32[512,4096]{1,0:T(8,128)} %bitcast.6, bf16[32,256,128]{2,1,0:T(8,128)(2,1)S(1)} %bitcast.4, s32[32]{0:T(128)S(1)} %bitcast.5, f32[288]{0:T(512)S(1)} %reshape.9.coef_in, s32[256]{0:T(256)S(1)} %reshape.10.index_in, s32[256]{0:T(256)S(1)} %reshape.11.cover_in), custom_call_target="tpu_custom_call" | custom-call | tf_op jit(solution)/shard_map/pallas_call | solution.py:391
  97.2 3.4 %shard_map.74 = f32[512,4096]{1,0:T(8,128)} custom-call(f32[512,4096]{1,0:T(8,128)S(1)} %shard_map.73.value), custom_call_target="tpu_custom_call" | custom-call | tf_op jit(solution)/shard_map/pallas_call | solution.py:418
Async XLA Ops:
  2.7 1.6 %copy-start = (bf16[1,32,256,128]{3,2,1,0:T(8,128)(2,1)S(1)}, bf16[1,32,256,128]{3,2,1,0:T(8,128)(2,1)}, u32[]{:S(2)}) copy-start(bf16[1,32,256,128]{3,2,1,0:T(8,128)(2,1)} %param.8) | copy-start | bytes 6291460
  4.3 1.2 %copy-start.1 = (f32[512,512]{1,0:T(8,128)S(1)}, f32[512,512]{1,0:T(8,128)}, u32[]{:S(2)}) copy-start(f32[512,512]{1,0:T(8,128)} %template.1) | copy-start | bytes 3145732
  5.5 0.7 copy-start.2

commit v2 on v1

--- a/solution.py
+++ b/solution.py
@@ -228,12 +228,12 @@
             pixels[j] = lines[slot, :, j * block : (j + 1) * block].astype(jnp.bfloat16)
         here = pl.ds(pl.multiple_of(i * LINES, LINES), LINES)
         for j in range(blocks):
-            start = offsets[j]
+            start = offsets[0, j]
             window = [pixels[start + k] for k in range(depth // block)]
             value = jnp.dot(
                 jnp.concatenate(window, axis=1), mats[j], preferred_element_type=jnp.float32
             )
-            covered = cover[me * (ccd_count * count) + row * count + j * block // patch_cols]
+            covered = cover[me, row, j * block // patch_cols]
             out[here, j * block : (j + 1) * block] = value * covered.astype(jnp.float32)
         return carry
 
@@ -246,14 +246,13 @@
     )
     weights[...] = jnp.zeros(weights.shape, jnp.float32)
     for q in range(count):
-        spot = me * (ccd_count * count) + row * count + q
-        chosen = index[spot]
-        covered = cover[spot].astype(jnp.float32)
+        chosen = index[me, row, q]
+        covered = cover[me, row, q].astype(jnp.float32)
         here = slice(EDGE + q * patch_cols, EDGE + (q + 1) * patch_cols)
         for b in range(3):
             terms = []
             for k in range(3):
-                sets = [coef[me * (KSETS * 9) + i * 9 + b * 3 + k] for i in range(KSETS)]
+                sets = [coef[b, k, i, me] for i in range(KSETS)]
                 term = sets[0]
                 for i in range(1, KSETS):
                     term = jnp.where(chosen == i, sets[i], term)
@@ -384,8 +383,12 @@
     patch_cols = template.shape[1]
     count, ccd_count = lax.axis_size("tile"), lax.axis_size("ccd")
     blocks, depth, block = interp.shape[1:]
-    small = [coef_table.reshape(-1), coef_index.reshape(-1), intersection.reshape(-1)]
-
+    small = [col_offsets, coef_table.transpose(2, 3, 1, 0), coef_index, intersection]
+
+    sources = [
+        pltpu.with_memory_space_constraint(array, pltpu.HBM)
+        for array in (template, exposures[0], interp[0], *small)
+    ]
     in_hbm = pl.BlockSpec(memory_space=pltpu.HBM)
     vmem = pl.BlockSpec(memory_space=pltpu.VMEM)
     value = pl.pallas_call(
@@ -401,7 +404,6 @@
             pltpu.VMEM((2, LINES, cols), jnp.float32),
             pltpu.VMEM((blocks, LINES, block), jnp.bfloat16),
             pltpu.VMEM((blocks, depth, block), jnp.bfloat16),
-            pltpu.SMEM((blocks,), jnp.int32),
             *[pltpu.SMEM(array.shape, array.dtype) for array in small],
             pltpu.SemaphoreType.DMA,
             pltpu.SemaphoreType.DMA((2,)),
@@ -414,7 +416,7 @@
         compiler_params=pltpu.CompilerParams(
             collective_id=0, has_side_effects=True, vmem_limit_bytes=40 * 2**20
         ),
-    )(template, exposures[0], interp[0], col_offsets[0], *small)
+    )(*sources)
     result = pl.pallas_call(
         store_kernel,
         out_shape=jax.ShapeDtypeStruct((rows, cols), jnp.float32),

time: 101 us -> 94.8 us (0.939)
  local copies, waits for them, and re-layouts: 6.14 us -> 0 us
    unnamed x7 -> x0, local copies, waits for them, and re-layouts: 4.34 us -> none
    reshape x3 -> x0, local copies, waits for them, and re-layouts: 1.8 us -> none  [the longest x1 0.81 us: on_device(): intersection.reshape(-1)]
where the time goes in v2:
time: 94.8 us; the launch traced here: 94.6 us
  Pallas kernels  94.6 us (100%)
    pallas_call x1, Pallas kernels, on_device(): pl.pallas_call(functools.partial(strip_kernel, count, ccd_count), out_sha...  91.2 us
    pallas_call x1, Pallas kernels, on_device(): pl.pallas_call(store_kernel, out_shape=jax.ShapeDtypeStruct((rows, cols),...  3.37 us

profile of v2, /device:TPU:1, one launch (start us, length us, event | category | flops | bytes accessed | tf_op | source)
XLA Modules:
  0.0 94.6 jit_solution(4675040527289432785)
XLA Ops:
  0.0 91.2 %shard_map.73.value = f32[512,4096]{1,0:T(8,128)S(1)} custom-call(f32[512,512]{1,0:T(8,128)} %template.1, f32[512,4096]{1,0:T(8,128)} %bitcast.4, bf16[32,256,128]{2,1,0:T(8,128)(2,1)} %bitcast.5, s32[1,32]{1,0:T(1,128)} %offset_in.1, f32[3,3,4,8]{3,2,1,0:T(4,128)} %bitcast.6, s32[8,4,8]{2,1,0:T(4,128)} %index_in.1, s32[8,4,8]{2,1,0:T(4,128)} %cover_in.1), custom_call_target="tpu_custom_call" | custom-call | tf_op jit(solution)/shard_map/pallas_call | solution.py:394
  91.3 3.4 %shard_map.74 = f32[512,4096]{1,0:T(8,128)} custom-call(f32[512,4096]{1,0:T(8,128)S(1)} %shard_map.73.value), custom_call_target="tpu_custom_call" | custom-call | tf_op jit(solution)/shard_map/pallas_call | solution.py:420

commit v3 on v2

--- a/solution.py
+++ b/solution.py
@@ -16,9 +16,10 @@
 HALO = 16
 EDGE = 128
 BAND = 128
-CHUNKS = 2
+MARGIN = 2
+NOTHING = 3
+CHUNKS = 4
 LINES = 128
-STORES = 8
 
 
 def basis_taps():
@@ -77,51 +78,103 @@
     )
 
 
-def arrival_events(count):
+def place(c):
+    return c + (c // 2) * (5 - 2 * c)
+
+
+def programs(count):
     inner = inner_size(count)
     steps = (-inner, inner, -1, 1)
     free, order = {}, 0
     queue = [(0, False, me, me, c, me * CHUNKS + c) for me in range(count) for c in range(CHUNKS)]
     order = len(queue)
     heapq.heapify(queue)
-    events = [[] for _ in range(count)]
+    arrivals = [[] for _ in range(count)]
+    drains = [[] for _ in range(count)]
     while queue:
         time, _, me, q, c, _ = heapq.heappop(queue)
         if q != me:
-            events[me].append(q * CHUNKS + c)
+            arrivals[me].append((time, q * CHUNKS + c))
+        sent = [time] if c % 2 == 0 else []
         for d, go in enumerate(paths(me, q, c, count)):
             if go:
                 done = max(free.get((me, d), 0), time) + 1
                 free[me, d] = done
+                sent.append(done)
                 to = me + steps[d]
                 heapq.heappush(queue, (done, (q - to) % inner != 0, to, q, c, order))
                 order += 1
-    return events
-
-
-DIGIT = 256
-PER_WORD = 3
-
-
-def arrival_codes(count):
-    codes = []
-    for events in arrival_events(count):
-        assert len(events) == (count - 1) * CHUNKS
+        if sent:
+            drains[me].append((max(sent) + MARGIN, q * CHUNKS + c))
+    result = []
+    for me in range(count):
         left = {q: CHUNKS for q in range(count)}
-        digits = []
-        for event in events:
+        steps = []
+        for i, (time, event) in enumerate(arrivals[me]):
             left[event // CHUNKS] -= 1
-            digits.append(event * 2 + (left[event // CHUNKS] == 0))
-        codes.append([
-            sum(int(v) * DIGIT**i for i, v in enumerate(digits[first : first + PER_WORD]))
-            for first in range(0, len(digits), PER_WORD)
-        ])
-    return codes
+            steps.append((time, 0, i, event * 4 + 2 * (left[event // CHUNKS] == 0)))
+        for i, (time, event) in enumerate(drains[me]):
+            steps.append((time, 1, i, event * 4 + 1))
+        result.append([step[-1] for step in sorted(steps)])
+    longest = max(len(steps) for steps in result)
+    finals = [arrivals[me][-1][1] // CHUNKS for me in range(count)]
+    return [steps + [NOTHING] * (longest - len(steps)) for steps in result], finals
+
+
+def pick(me, values):
+    value = jnp.int32(values[0])
+    for i in range(1, len(values)):
+        value = jnp.where(me == i, jnp.int32(values[i]), value)
+    return value
+
+
+def codes(count):
+    digit, per_word = (128, 4) if count * CHUNKS * 4 <= 128 else (256, 3)
+    steps, finals = programs(count)
+    words = [
+        [sum(v * digit**i for i, v in enumerate(line[first : first + per_word])) for line in steps]
+        for first in range(0, len(steps[0]), per_word)
+    ]
+    return words, digit, per_word, len(steps[0]), finals
+
+
+def spans(q, patch_cols, cols):
+    first = pl.multiple_of(q * patch_cols, EDGE)
+    left = pl.multiple_of(jnp.maximum(first - EDGE, 0), EDGE)
+    right = pl.multiple_of(jnp.minimum(first + patch_cols, cols - EDGE), EDGE)
+    return (
+        (pl.ds(left, EDGE), slice(0, EDGE)),
+        (pl.ds(first, patch_cols), slice(EDGE, EDGE + patch_cols)),
+        (pl.ds(right, EDGE), slice(EDGE + patch_cols, 2 * EDGE + patch_cols)),
+    )
+
+
+def band_model(q, r, rows, strip, down, across, weights):
+    patch_cols = strip.shape[2]
+    first = pl.multiple_of(q * patch_cols, EDGE)
+    wide = patch_cols + 2 * EDGE
+    at = pl.multiple_of(r * BAND, BAND)
+    pixel = strip[q, pl.ds(at, BAND + 2 * HALO), :].astype(jnp.bfloat16)
+    tall = jnp.dot(down[...], pixel, preferred_element_type=jnp.float32)
+    tall = tall.astype(jnp.bfloat16)
+    v = (
+        lax.broadcasted_iota(jnp.int32, (BAND, wide), 0) + r * BAND
+    ).astype(jnp.float32) * (2.0 / rows) - (rows - 1) / rows
+    model = None
+    for b in range(3):
+        flat = jnp.dot(
+            tall[b * BAND : (b + 1) * BAND], across[b], preferred_element_type=jnp.float32
+        )
+        const = weights[b : b + 1, pl.ds(first, wide)]
+        slope = weights[3 + b : 4 + b, pl.ds(first, wide)]
+        term = (const + slope * v) * flat
+        model = term if model is None else model + term
+    return model
 
 
 def strip_kernel(
-    count, ccd_count, template, exposure, interp, offset_in, coef_in, index_in, cover_in, out,
-    strip, down, across, weights, lines, pixels, mats, offsets, coef, index, cover,
+    count, ccd_count, template, exposure, interp, offset_in, coef_in, index_in, cover_in,
+    out, strip, down, across, weights, lines, pixels, mats, offsets, coef, index, cover,
     load_sem, line_sem, small_sem, send_sem, recv_sem, hsend_sem, hrecv_sem,
 ):
     me = lax.axis_index("tile")
@@ -170,9 +223,10 @@
     pl.semaphore_wait(barrier, total)
 
     def send(q, c, d, own):
-        piece = pl.ds(pl.multiple_of(HALO + c * part, HALO), part)
+        first = place(c) * part
+        piece = pl.ds(pl.multiple_of(HALO + first, HALO), part)
         return pltpu.make_async_remote_copy(
-            src_ref=template.at[pl.ds(c * part, part)] if own else strip.at[q, piece],
+            src_ref=template.at[pl.ds(first, part)] if own else strip.at[q, piece],
             dst_ref=strip.at[q, piece],
             send_sem=send_sem.at[d, q, c],
             recv_sem=recv_sem.at[q, c],
@@ -262,32 +316,11 @@
             weights[3 + b : 4 + b, here] = jnp.full((1, patch_cols), lift, jnp.float32)
 
     def add_model(q):
-        first = pl.multiple_of(q * patch_cols, EDGE)
-        wide = patch_cols + 2 * EDGE
-        left = pl.multiple_of(jnp.maximum(first - EDGE, 0), EDGE)
-        right = pl.multiple_of(jnp.minimum(first + patch_cols, cols - EDGE), EDGE)
-
         def band(r, carry):
-            at = pl.multiple_of(r * BAND, BAND)
-            here = pl.ds(at, BAND)
-            pixel = strip[q, pl.ds(at, BAND + 2 * HALO), :].astype(jnp.bfloat16)
-            tall = jnp.dot(down[...], pixel, preferred_element_type=jnp.float32)
-            tall = tall.astype(jnp.bfloat16)
-            v = (
-                lax.broadcasted_iota(jnp.int32, (BAND, wide), 0) + r * BAND
-            ).astype(jnp.float32) * (2.0 / rows) - (rows - 1) / rows
-            model = None
-            for b in range(3):
-                flat = jnp.dot(
-                    tall[b * BAND : (b + 1) * BAND], across[b], preferred_element_type=jnp.float32
-                )
-                const = weights[b : b + 1, pl.ds(first, wide)]
-                slope = weights[3 + b : 4 + b, pl.ds(first, wide)]
-                term = (const + slope * v) * flat
-                model = term if model is None else model + term
-            out[here, pl.ds(first, patch_cols)] -= model[:, EDGE : EDGE + patch_cols]
-            out[here, pl.ds(left, EDGE)] -= model[:, :EDGE]
-            out[here, pl.ds(right, EDGE)] -= model[:, EDGE + patch_cols :]
+            model = band_model(q, r, rows, strip, down, across, weights)
+            here = pl.ds(pl.multiple_of(r * BAND, BAND), BAND)
+            for there, piece in spans(q, patch_cols, cols):
+                out[here, there] -= model[:, piece]
             return carry
 
         lax.fori_loop(0, rows // BAND, band, 0)
@@ -313,69 +346,104 @@
     halos_in(me)
     add_model(me)
 
-    table = arrival_codes(count)
-    words = []
-    for w in range(len(table[0])):
-        word = jnp.int32(0)
-        for i in range(count):
-            word = jnp.where(me == i, jnp.int32(table[i][w]), word)
-        words.append(word)
-
-    def arrive(_, words):
+    table, digit, per_word, length, finals = codes(count)
+    final = pick(me, finals)
+
+    def step(_, words):
         words = list(words)
-        digit = words[0] % DIGIT
+        code = words[0] % digit
         for w in range(len(words)):
-            words[w] = words[w] // DIGIT
+            words[w] = words[w] // digit
             if w + 1 < len(words):
-                words[w] = words[w] + (words[w + 1] % DIGIT) * DIGIT ** (PER_WORD - 1)
-        done, event = digit % 2, digit // 2
-        q, c = event // CHUNKS, event % CHUNKS
-        send(q, c, 0, False).wait_recv()
-        onward = paths(me, q, c, count)
-        for d in range(4):
-            @pl.when(onward[d])
-            def _():
-                send(q, c, d, False).start()
-        for d in range(2):
-            @pl.when((c == (0 if d == 0 else CHUNKS - 1)) & halo_there[d])
-            def _():
-                halo(q, d).start()
-
-        @pl.when(done == 1)
-        def _():
-            halos_in(q)
-            add_model(q)
-
-        return tuple(words)
-
-    lax.fori_loop(0, (count - 1) * CHUNKS, arrive, tuple(words))
-
-    def drain(event, carry):
+                words[w] = words[w] + (words[w + 1] % digit) * digit ** (per_word - 1)
+        kind, event = code % 4, code // 4
         q, c = event // CHUNKS, event % CHUNKS
         onward = paths(me, q, c, count)
-        for d in range(4):
-            @pl.when(onward[d])
-            def _():
-                send(q, c, d, False).wait_send()
-        for d in range(2):
-            @pl.when((c == 0) & halo_there[d])
-            def _():
-                halo(q, d).wait_send()
-        return carry
-
-    lax.fori_loop(0, count * CHUNKS, drain, 0)
-
-
-def store_kernel(value, out, sem):
-    rows = value.shape[0] // STORES
-    copies = [
-        pltpu.make_async_copy(value.at[pl.ds(i * rows, rows)], out.at[pl.ds(i * rows, rows)], sem.at[i])
-        for i in range(STORES)
-    ]
-    for copy in copies:
-        copy.start()
-    for copy in copies:
-        copy.wait()
+        halos = [(c == 2 * d) & halo_there[d] for d in range(2)]
+
+        @pl.when(kind % 2 == 0)
+        def _():
+            send(q, c, 0, False).wait_recv()
+            for d in range(4):
+                @pl.when(onward[d])
+                def _():
+                    send(q, c, d, False).start()
+            for d in range(2):
+                @pl.when(halos[d])
+                def _():
+                    halo(q, d).start()
+
+        @pl.when(kind == 2)
+        def _():
+            halos_in(q)
+
+            @pl.when(q != final)
+            def _():
+                add_model(q)
+
+        @pl.when(kind == 1)
+        def _():
+            for d in range(4):
+                @pl.when(onward[d])
+                def _():
+                    send(q, c, d, False).wait_send()
+            for d in range(2):
+                @pl.when(halos[d])
+                def _():
+                    halo(q, d).wait_send()
+
+        return tuple(words)
+
+    lax.fori_loop(0, length, step, tuple(pick(me, line) for line in table))
+
+
+def finish_kernel(count, strip, down, across, weights, value, out, work, far_sem, near_sem):
+    rows, cols = value.shape
+    patch_cols = strip.shape[2]
+    final = pick(lax.axis_index("tile"), codes(count)[-1])
+    pieces = spans(final, patch_cols, cols)
+    within = (final > 0, final >= 0, final < count - 1)
+
+    def far(q, shift, size):
+        here = (slice(None), pl.ds(q * patch_cols + shift, size))
+        return pltpu.make_async_copy(value.at[here], out.at[here], far_sem.at[q])
+
+    def near(i, r):
+        there, piece = pieces[i]
+        return pltpu.make_async_copy(
+            work.at[pl.ds(r * BAND, BAND), piece], out.at[pl.ds(r * BAND, BAND), there], near_sem.at[i, r]
+        )
+
+    def far_copies(act):
+        for q in range(count):
+            @pl.when((q < final - 1) | (q > final + 1))
+            def _():
+                act(far(q, 0, patch_cols))
+
+            @pl.when(q == final - 1)
+            def _():
+                act(far(q, 0, patch_cols - EDGE))
+
+            @pl.when(q == final + 1)
+            def _():
+                act(far(q, EDGE, patch_cols - EDGE))
+
+    far_copies(lambda copy: copy.start())
+    for r in range(rows // BAND):
+        model = band_model(final, r, rows, strip, down, across, weights)
+        here = pl.ds(r * BAND, BAND)
+        for i, (there, piece) in enumerate(pieces):
+            work[here, piece] = value[here, there] - model[:, piece]
+
+            @pl.when(within[i])
+            def _():
+                near(i, r).start()
+    far_copies(lambda copy: copy.wait())
+    for r in range(rows // BAND):
+        for i in range(3):
+            @pl.when(within[i])
+            def _():
+                near(i, r).wait()
 
 
 def on_device(exposures, interp, col_offsets, template, coef_table, coef_index, intersection):
@@ -391,16 +459,19 @@
     ]
     in_hbm = pl.BlockSpec(memory_space=pltpu.HBM)
     vmem = pl.BlockSpec(memory_space=pltpu.VMEM)
-    value = pl.pallas_call(
+    shapes = [
+        ((rows, cols), jnp.float32),
+        ((count, rows + 2 * HALO, patch_cols), jnp.float32),
+        ((3 * BAND, BAND + 2 * HALO), jnp.bfloat16),
+        ((3, patch_cols, patch_cols + 2 * EDGE), jnp.bfloat16),
+        ((8, cols + 2 * EDGE), jnp.float32),
+    ]
+    value, strip, down, across, weights = pl.pallas_call(
         functools.partial(strip_kernel, count, ccd_count),
-        out_shape=jax.ShapeDtypeStruct((rows, cols), jnp.float32),
+        out_shape=[jax.ShapeDtypeStruct(*shape) for shape in shapes],
         in_specs=[in_hbm] * 7,
-        out_specs=vmem,
+        out_specs=[vmem] * 5,
         scratch_shapes=[
-            pltpu.VMEM((count, rows + 2 * HALO, patch_cols), jnp.float32),
-            pltpu.VMEM((3 * BAND, BAND + 2 * HALO), jnp.bfloat16),
-            pltpu.VMEM((3, patch_cols, patch_cols + 2 * EDGE), jnp.bfloat16),
-            pltpu.VMEM((8, cols + 2 * EDGE), jnp.float32),
             pltpu.VMEM((2, LINES, cols), jnp.float32),
             pltpu.VMEM((blocks, LINES, block), jnp.bfloat16),
             pltpu.VMEM((blocks, depth, block), jnp.bfloat16),
@@ -414,17 +485,21 @@
             pltpu.SemaphoreType.DMA((2, count)),
         ],
         compiler_params=pltpu.CompilerParams(
-            collective_id=0, has_side_effects=True, vmem_limit_bytes=40 * 2**20
+            collective_id=0, has_side_effects=True, vmem_limit_bytes=16 * 2**20
         ),
     )(*sources)
     result = pl.pallas_call(
-        store_kernel,
+        functools.partial(finish_kernel, count),
         out_shape=jax.ShapeDtypeStruct((rows, cols), jnp.float32),
-        in_specs=[vmem],
+        in_specs=[vmem] * 5,
         out_specs=in_hbm,
-        scratch_shapes=[pltpu.SemaphoreType.DMA((STORES,))],
-        compiler_params=pltpu.CompilerParams(vmem_limit_bytes=2**20),
-    )(value)
+        scratch_shapes=[
+            pltpu.VMEM((rows, patch_cols + 2 * EDGE), jnp.float32),
+            pltpu.SemaphoreType.DMA((count,)),
+            pltpu.SemaphoreType.DMA((3, rows // BAND)),
+        ],
+        compiler_params=pltpu.CompilerParams(vmem_limit_bytes=16 * 2**20),
+    )(strip, down, across, weights, value)
     return result[None]
 
 

time: 94.8 us -> 89.9 us (0.948)
  Pallas kernels: 94.6 us -> 88.9 us
    pallas_call x1, Pallas kernels: 91.2 us -> 85.4 us  [on_device(): pl.pallas_call(functools.partial(strip_kernel, count, ccd_count), out_sha...]
where the time goes in v3:
time: 89.9 us; the launch traced here: 88.9 us
  Pallas kernels  88.9 us (99%)
    pallas_call x1, Pallas kernels, on_device(): pl.pallas_call(functools.partial(strip_kernel, count, ccd_count), out_sha...  85.4 us
    pallas_call x1, Pallas kernels, on_device(): pl.pallas_call(functools.partial(finish_kernel, count), out_shape=jax.Sha...  3.51 us

profile of v3, /device:TPU:1, one launch (start us, length us, event | category | flops | bytes accessed | tf_op | source)
XLA Modules:
  0.0 88.9 jit_solution(2860852730074160606)
XLA Ops:
  0.0 85.4 %shard_map.73 = (f32[512,4096]{1,0:T(8,128)S(1)}, f32[8,544,512]{2,1,0:T(8,128)S(1)}, bf16[384,160]{1,0:T(8,128)(2,1)S(1)}, bf16[3,512,768]{2,1,0:T(8,128)(2,1)S(1)}, f32[8,4352]{1,0:T(8,128)S(1)}) custom-call(f32[512,512]{1,0:T(8,128)} %template.1, f32[512,4096]{1,0:T(8,128)} %bitcast.4, bf16[32,256,128]{2,1,0:T(8,128)(2,1)} %bitcast.5, s32[1,32]{1,0:T(1,128)} %offset_in.1, ...), custom_call_target="tpu_custom_call" | custom-call | tf_op jit(solution)/shard_map/pallas_call | solution.py:469
  85.4 3.5 %shard_map.74 = f32[512,4096]{1,0:T(8,128)} custom-call(f32[8,544,512]{2,1,0:T(8,128)S(1)} %get-tuple-element.10.strip, bf16[384,160]{1,0:T(8,128)(2,1)S(1)} %get-tuple-element.11.down, bf16[3,512,768]{2,1,0:T(8,128)(2,1)S(1)} %get-tuple-element.12.across, f32[8,4352]{1,0:T(8,128)S(1)} %get-tuple-element.13.weights, f32[512,4096]{1,0:T(8,128)S(1)} %get-tuple-element.14.value), custom_call_target="tpu_custom_call" | custom-call | tf_op jit(solution)/shard_map/pallas_call | solution.py:491

commit v4 on v3

--- a/solution.py
+++ b/solution.py
@@ -16,7 +16,7 @@
 HALO = 16
 EDGE = 128
 BAND = 128
-MARGIN = 2
+MARGIN = 1
 NOTHING = 3
 CHUNKS = 4
 LINES = 128
@@ -79,7 +79,8 @@
 
 
 def place(c):
-    return c + (c // 2) * (5 - 2 * c)
+    half = CHUNKS // 2
+    return c + (c // half) * (CHUNKS + half - 1 - 2 * c)
 
 
 def programs(count):
@@ -95,7 +96,7 @@
         time, _, me, q, c, _ = heapq.heappop(queue)
         if q != me:
             arrivals[me].append((time, q * CHUNKS + c))
-        sent = [time] if c % 2 == 0 else []
+        sent = [time] if c % (CHUNKS // 2) == 0 else []
         for d, go in enumerate(paths(me, q, c, count)):
             if go:
                 done = max(free.get((me, d), 0), time) + 1
@@ -118,7 +119,7 @@
         result.append([step[-1] for step in sorted(steps)])
     longest = max(len(steps) for steps in result)
     finals = [arrivals[me][-1][1] // CHUNKS for me in range(count)]
-    return [steps + [NOTHING] * (longest - len(steps)) for steps in result], finals
+    return [[NOTHING] * (longest - len(steps)) + steps for steps in result], finals
 
 
 def pick(me, values):
@@ -129,7 +130,8 @@
 
 
 def codes(count):
-    digit, per_word = (128, 4) if count * CHUNKS * 4 <= 128 else (256, 3)
+    bits = (count * CHUNKS * 4 - 1).bit_length()
+    digit, per_word = 2**bits, 30 // bits
     steps, finals = programs(count)
     words = [
         [sum(v * digit**i for i, v in enumerate(line[first : first + per_word])) for line in steps]
@@ -203,6 +205,35 @@
             pl.semaphore_signal(barrier, inc=1, device_id=(row + step, me))
         total = total + exists.astype(jnp.int32)
 
+    pl.semaphore_wait(barrier, total)
+
+    def send(q, c, d, own):
+        first = place(c) * part
+        piece = pl.ds(pl.multiple_of(HALO + first, HALO), part)
+        return pltpu.make_async_remote_copy(
+            src_ref=template.at[pl.ds(first, part)] if own else strip.at[q, piece],
+            dst_ref=strip.at[q, piece],
+            send_sem=send_sem.at[d, q, c],
+            recv_sem=recv_sem.at[q, c],
+            device_id=(row, targets[d]),
+        )
+
+    def halo(q, d):
+        source = pl.ds(HALO, HALO) if d == 0 else pl.ds(rows, HALO)
+        target = pl.ds(HALO + rows, HALO) if d == 0 else pl.ds(0, HALO)
+        return pltpu.make_async_remote_copy(
+            src_ref=strip.at[q, source],
+            dst_ref=strip.at[q, target],
+            send_sem=hsend_sem.at[d, q],
+            recv_sem=hrecv_sem.at[d, q],
+            device_id=(row + (-1 if d == 0 else 1), me),
+        )
+
+    for c in range(CHUNKS):
+        for d in range(4):
+            @pl.when(there[d])
+            def _():
+                send(me, c, d, True).start()
     load = pltpu.make_async_copy(template, strip.at[me, pl.ds(HALO, rows)], load_sem)
     load.start()
     small = [
@@ -220,35 +251,6 @@
         )
 
     line_copy(0, 0).start()
-    pl.semaphore_wait(barrier, total)
-
-    def send(q, c, d, own):
-        first = place(c) * part
-        piece = pl.ds(pl.multiple_of(HALO + first, HALO), part)
-        return pltpu.make_async_remote_copy(
-            src_ref=template.at[pl.ds(first, part)] if own else strip.at[q, piece],
-            dst_ref=strip.at[q, piece],
-            send_sem=send_sem.at[d, q, c],
-            recv_sem=recv_sem.at[q, c],
-            device_id=(row, targets[d]),
-        )
-
-    def halo(q, d):
-        source = pl.ds(HALO, HALO) if d == 0 else pl.ds(rows, HALO)
-        target = pl.ds(HALO + rows, HALO) if d == 0 else pl.ds(0, HALO)
-        return pltpu.make_async_remote_copy(
-            src_ref=strip.at[q, source],
-            dst_ref=strip.at[q, target],
-            send_sem=hsend_sem.at[d, q],
-            recv_sem=hrecv_sem.at[d, q],
-            device_id=(row + (-1 if d == 0 else 1), me),
-        )
-
-    for c in range(CHUNKS):
-        for d in range(4):
-            @pl.when(there[d])
-            def _():
-                send(me, c, d, True).start()
     load.wait()
     for d in range(2):
         @pl.when(halo_there[d])
@@ -359,19 +361,19 @@
         kind, event = code % 4, code // 4
         q, c = event // CHUNKS, event % CHUNKS
         onward = paths(me, q, c, count)
-        halos = [(c == 2 * d) & halo_there[d] for d in range(2)]
+        halos = [(c == CHUNKS // 2 * d) & halo_there[d] for d in range(2)]
 
         @pl.when(kind % 2 == 0)
         def _():
             send(q, c, 0, False).wait_recv()
+            for d in range(2):
+                @pl.when(halos[d])
+                def _():
+                    halo(q, d).start()
             for d in range(4):
                 @pl.when(onward[d])
                 def _():
                     send(q, c, d, False).start()
-            for d in range(2):
-                @pl.when(halos[d])
-                def _():
-                    halo(q, d).start()
 
         @pl.when(kind == 2)
         def _():

time: 89.9 us -> 89.9 us (level)
  no operation moved by 1% of the time
where the time goes in v4:
time: 89.9 us; the launch traced here: 88.8 us
  Pallas kernels  88.8 us (99%)
    pallas_call x1, Pallas kernels, on_device(): pl.pallas_call(functools.partial(strip_kernel, count, ccd_count), out_sha...  85.3 us
    pallas_call x1, Pallas kernels, on_device(): pl.pallas_call(functools.partial(finish_kernel, count), out_shape=jax.Sha...  3.51 us

profile of v4, /device:TPU:1, one launch (start us, length us, event | category | flops | bytes accessed | tf_op | source)
XLA Modules:
  0.0 88.8 jit_solution(18155712667976436478)
XLA Ops:
  0.0 85.3 %shard_map.73 = (f32[512,4096]{1,0:T(8,128)S(1)}, f32[8,544,512]{2,1,0:T(8,128)S(1)}, bf16[384,160]{1,0:T(8,128)(2,1)S(1)}, bf16[3,512,768]{2,1,0:T(8,128)(2,1)S(1)}, f32[8,4352]{1,0:T(8,128)S(1)}) custom-call(f32[512,512]{1,0:T(8,128)} %template.1, f32[512,4096]{1,0:T(8,128)} %bitcast.4, bf16[32,256,128]{2,1,0:T(8,128)(2,1)} %bitcast.5, s32[1,32]{1,0:T(1,128)} %offset_in.1, ...), custom_call_target="tpu_custom_call" | custom-call | tf_op jit(solution)/shard_map/pallas_call | solution.py:471
  85.3 3.5 %shard_map.74 = f32[512,4096]{1,0:T(8,128)} custom-call(f32[8,544,512]{2,1,0:T(8,128)S(1)} %get-tuple-element.10.strip, bf16[384,160]{1,0:T(8,128)(2,1)S(1)} %get-tuple-element.11.down, bf16[3,512,768]{2,1,0:T(8,128)(2,1)S(1)} %get-tuple-element.12.across, f32[8,4352]{1,0:T(8,128)S(1)} %get-tuple-element.13.weights, f32[512,4096]{1,0:T(8,128)S(1)} %get-tuple-element.14.value), custom_call_target="tpu_custom_call" | custom-call | tf_op jit(solution)/shard_map/pallas_call | solution.py:493

commit v5 on v4

--- a/solution.py
+++ b/solution.py
@@ -192,6 +192,9 @@
     there = (z > 0, z < outer - 1, x > 0, x < inner - 1)
     halo_there = (row > 0, row < ccd_count - 1)
 
+    load = pltpu.make_async_copy(template, strip.at[me, pl.ds(HALO, rows)], load_sem)
+    load.start()
+
     barrier = pltpu.get_barrier_semaphore()
     total = jnp.int32(0)
     for target, exists in zip(targets, there):
@@ -205,13 +208,14 @@
             pl.semaphore_signal(barrier, inc=1, device_id=(row + step, me))
         total = total + exists.astype(jnp.int32)
 
+    load.wait()
     pl.semaphore_wait(barrier, total)
 
-    def send(q, c, d, own):
+    def send(q, c, d):
         first = place(c) * part
         piece = pl.ds(pl.multiple_of(HALO + first, HALO), part)
         return pltpu.make_async_remote_copy(
-            src_ref=template.at[pl.ds(first, part)] if own else strip.at[q, piece],
+            src_ref=strip.at[q, piece],
             dst_ref=strip.at[q, piece],
             send_sem=send_sem.at[d, q, c],
             recv_sem=recv_sem.at[q, c],
@@ -230,12 +234,10 @@
         )
 
     for c in range(CHUNKS):
-        for d in range(4):
+        for d in (2, 3, 0, 1):
             @pl.when(there[d])
             def _():
-                send(me, c, d, True).start()
-    load = pltpu.make_async_copy(template, strip.at[me, pl.ds(HALO, rows)], load_sem)
-    load.start()
+                send(me, c, d).start()
     small = [
         pltpu.make_async_copy(source, target, small_sem.at[i])
         for i, (source, target) in enumerate(
@@ -251,7 +253,6 @@
         )
 
     line_copy(0, 0).start()
-    load.wait()
     for d in range(2):
         @pl.when(halo_there[d])
         def _():
@@ -365,30 +366,30 @@
 
         @pl.when(kind % 2 == 0)
         def _():
-            send(q, c, 0, False).wait_recv()
+            send(q, c, 0).wait_recv()
             for d in range(2):
                 @pl.when(halos[d])
                 def _():
                     halo(q, d).start()
+            for d in (2, 3, 0, 1):
+                @pl.when(onward[d])
+                def _():
+                    send(q, c, d).start()
+
+        @pl.when(kind == 2)
+        def _():
+            halos_in(q)
+
+            @pl.when(q != final)
+            def _():
+                add_model(q)
+
+        @pl.when(kind == 1)
+        def _():
             for d in range(4):
                 @pl.when(onward[d])
                 def _():
-                    send(q, c, d, False).start()
-
-        @pl.when(kind == 2)
-        def _():
-            halos_in(q)
-
-            @pl.when(q != final)
-            def _():
-                add_model(q)
-
-        @pl.when(kind == 1)
-        def _():
-            for d in range(4):
-                @pl.when(onward[d])
-                def _():
-                    send(q, c, d, False).wait_send()
+                    send(q, c, d).wait_send()
             for d in range(2):
                 @pl.when(halos[d])
                 def _():

time: 89.9 us -> 89.7 us (level)
  no operation moved by 1% of the time
where the time goes in v5:
time: 89.7 us; the launch traced here: 88.6 us
  Pallas kernels  88.5 us (99%)
    pallas_call x1, Pallas kernels, on_device(): pl.pallas_call(functools.partial(strip_kernel, count, ccd_count), out_sha...  85 us
    pallas_call x1, Pallas kernels, on_device(): pl.pallas_call(functools.partial(finish_kernel, count), out_shape=jax.Sha...  3.51 us

profile of v5, /device:TPU:1, one launch (start us, length us, event | category | flops | bytes accessed | tf_op | source)
XLA Modules:
  0.0 88.6 jit_solution(14859662732420837900)
XLA Ops:
  0.0 85.0 %shard_map.73 = (f32[512,4096]{1,0:T(8,128)S(1)}, f32[8,544,512]{2,1,0:T(8,128)S(1)}, bf16[384,160]{1,0:T(8,128)(2,1)S(1)}, bf16[3,512,768]{2,1,0:T(8,128)(2,1)S(1)}, f32[8,4352]{1,0:T(8,128)S(1)}) custom-call(f32[512,512]{1,0:T(8,128)} %template.1, f32[512,4096]{1,0:T(8,128)} %bitcast.4, bf16[32,256,128]{2,1,0:T(8,128)(2,1)} %bitcast.5, s32[1,32]{1,0:T(1,128)} %offset_in.1, ...), custom_call_target="tpu_custom_call" | custom-call | tf_op jit(solution)/shard_map/pallas_call | solution.py:472
  85.0 3.5 %shard_map.74 = f32[512,4096]{1,0:T(8,128)} custom-call(f32[8,544,512]{2,1,0:T(8,128)S(1)} %get-tuple-element.10.strip, bf16[384,160]{1,0:T(8,128)(2,1)S(1)} %get-tuple-element.11.down, bf16[3,512,768]{2,1,0:T(8,128)(2,1)S(1)} %get-tuple-element.12.across, f32[8,4352]{1,0:T(8,128)S(1)} %get-tuple-element.13.weights, f32[512,4096]{1,0:T(8,128)S(1)} %get-tuple-element.14.value), custom_call_target="tpu_custom_call" | custom-call | tf_op jit(solution)/shard_map/pallas_call | solution.py:494

commit v6 on v5

--- a/solution.py
+++ b/solution.py
@@ -164,9 +164,16 @@
     ).astype(jnp.float32) * (2.0 / rows) - (rows - 1) / rows
     model = None
     for b in range(3):
-        flat = jnp.dot(
-            tall[b * BAND : (b + 1) * BAND], across[b], preferred_element_type=jnp.float32
-        )
+        parts = []
+        for at in range(0, wide, 2 * EDGE):
+            low = max(0, at - EDGE - HALF) // EDGE * EDGE
+            high = min(patch_cols, -(-(at + EDGE + HALF) // EDGE) * EDGE)
+            parts.append(jnp.dot(
+                tall[b * BAND : (b + 1) * BAND, low:high],
+                across[b, low:high, at : at + 2 * EDGE],
+                preferred_element_type=jnp.float32,
+            ))
+        flat = jnp.concatenate(parts, axis=1)
         const = weights[b : b + 1, pl.ds(first, wide)]
         slope = weights[3 + b : 4 + b, pl.ds(first, wide)]
         term = (const + slope * v) * flat

time: 89.7 us -> 89.7 us (level)
  no operation moved by 1% of the time
where the time goes in v6:
time: 89.7 us; the launch traced here: 88.6 us
  Pallas kernels  88.6 us (99%)
    pallas_call x1, Pallas kernels, on_device(): pl.pallas_call(functools.partial(strip_kernel, count, ccd_count), out_sha...  85 us
    pallas_call x1, Pallas kernels, on_device(): pl.pallas_call(functools.partial(finish_kernel, count), out_shape=jax.Sha...  3.51 us

profile of v6, /device:TPU:1, one launch (start us, length us, event | category | flops | bytes accessed | tf_op | source)
XLA Modules:
  0.0 88.6 jit_solution(16586309330768029233)
XLA Ops:
  0.0 85.0 %shard_map.73 = (f32[512,4096]{1,0:T(8,128)S(1)}, f32[8,544,512]{2,1,0:T(8,128)S(1)}, bf16[384,160]{1,0:T(8,128)(2,1)S(1)}, bf16[3,512,768]{2,1,0:T(8,128)(2,1)S(1)}, f32[8,4352]{1,0:T(8,128)S(1)}) custom-call(f32[512,512]{1,0:T(8,128)} %template.1, f32[512,4096]{1,0:T(8,128)} %bitcast.4, bf16[32,256,128]{2,1,0:T(8,128)(2,1)} %bitcast.5, s32[1,32]{1,0:T(1,128)} %offset_in.1, ...), custom_call_target="tpu_custom_call" | custom-call | tf_op jit(solution)/shard_map/pallas_call | solution.py:479
  85.0 3.5 %shard_map.74 = f32[512,4096]{1,0:T(8,128)} custom-call(f32[8,544,512]{2,1,0:T(8,128)S(1)} %get-tuple-element.10.strip, bf16[384,160]{1,0:T(8,128)(2,1)S(1)} %get-tuple-element.11.down, bf16[3,512,768]{2,1,0:T(8,128)(2,1)S(1)} %get-tuple-element.12.across, f32[8,4352]{1,0:T(8,128)S(1)} %get-tuple-element.13.weights, f32[512,4096]{1,0:T(8,128)S(1)} %get-tuple-element.14.value), custom_call_target="tpu_custom_call" | custom-call | tf_op jit(solution)/shard_map/pallas_call | solution.py:501
